TPU v7x, 32 devices: a whole 2x2x4 slice. The times are simulated.
32 devices in a mesh: shard: 8 (over z, core), batch: 4 (over y, x).
Axes of the slice: x: 2, y: 2, z: 4, core: 2. Of those that a mesh axis runs over, the one named last changes fastest.
Arguments:
- data_inputs: bfloat16 [8, 256, 1024], P('shard', 'batch'), may hold values from -6 to 6
- data_targets: bfloat16 [8, 256, 512], P('shard', 'batch'), may hold values from -6 to 6
- row_picks: int32 [2, 8, 512], P(None, 'shard', 'batch'), may hold values from 0 to 63
- layer_one: float32 [8, 1024, 2048], P('shard', None, 'batch'), may hold values from -6 to 6
- layer_two: float32 [8, 2048, 512], P('shard', 'batch'), may hold values from -6 to 6
- noise_one: bfloat16 [2, 8, 1024, 2048], P(None, 'shard', None, 'batch'), may hold values from -6 to 6
- noise_two: bfloat16 [2, 8, 2048, 512], P(None, 'shard', 'batch'), may hold values from -6 to 6
Outputs:
- moved_one: float32 [8, 1024, 2048], P('shard', None, 'batch')
- moved_two: float32 [8, 2048, 512], P('shard', 'batch')
- last_errors: bfloat16 [8, 512, 512], P('shard', 'batch')
All inputs are finite; a program needn't handle non-finite values.
Results may differ from a plain program's by a relative error of at most 0.014.
Values may be sent and summed in bfloat16 or wider, within the bound.
A program may use at most 64 MiB of HBM per device.

v0:
```python
import jax
import jax.numpy as jnp
from jax import lax
from jax.sharding import PartitionSpec as P

D_IN = 1024
HID = 2048
STEPS = 2


half_step = 0.01
root_step = 0.02**0.5
precision_obs = 32.0


def passed_along(value, axis, by):
    size = lax.axis_size(axis)
    return lax.ppermute(value, axis, [(i, (i + by) % size) for i in range(size)])


def per_device(data_inputs, data_targets, row_picks, layer_one, layer_two, noise_one, noise_two):
    scale_in = D_IN ** (-0.5)
    scale_hid = HID ** (-0.5)
    weights_a = layer_one[0]
    weights_b = layer_two[0]
    contract_rows = (((0,), (0,)), ((), ()))
    contract_cols = (((1,), (1,)), ((), ()))
    own_errors = jnp.zeros((row_picks.shape[2], weights_b.shape[1]), jnp.float32)
    for iteration in range(STEPS):
        chosen = row_picks[iteration, 0]
        local_rows = jnp.take(data_inputs[0], chosen, axis=0)
        local_targets = jnp.take(data_targets[0], chosen, axis=0)
        bf_a = weights_a.astype(jnp.bfloat16)
        bf_b = weights_b.astype(jnp.bfloat16)
        all_rows = lax.all_gather(local_rows, "batch", axis=0, tiled=True)
        hidden = jnp.tanh(jnp.dot(all_rows, bf_a, preferred_element_type=jnp.float32) * scale_in)
        hidden_b = hidden.astype(jnp.bfloat16)
        predicted = lax.psum_scatter(
            (jnp.dot(hidden_b, bf_b, preferred_element_type=jnp.float32) * scale_hid).astype(
                jnp.bfloat16
            ),
            "batch",
            scatter_dimension=0,
            tiled=True,
        ).astype(jnp.float32)
        own_errors = predicted - local_targets.astype(jnp.float32)
        signal = lax.all_gather(
            (precision_obs * own_errors).astype(jnp.bfloat16), "batch", axis=0, tiled=True
        )
        grad_two = (
            lax.dot_general(hidden_b, signal, contract_rows, preferred_element_type=jnp.float32)
            * scale_hid
        )
        back_hidden = (
            lax.dot_general(signal, bf_b, contract_cols, preferred_element_type=jnp.float32)
            * scale_hid
            * (1.0 - hidden * hidden)
        ).astype(jnp.bfloat16)
        grad_one = (
            lax.dot_general(
                all_rows, back_hidden, contract_rows, preferred_element_type=jnp.float32
            )
            * scale_in
        )
        weights_a = (
            weights_a
            - half_step * (grad_one + weights_a)
            + root_step * noise_one[iteration, 0].astype(jnp.float32)
        )
        weights_b = (
            weights_b
            - half_step * (grad_two + weights_b)
            + root_step * noise_two[iteration, 0].astype(jnp.float32)
        )
    moved_a, moved_b = (
        passed_along(weights_a.astype(jnp.bfloat16), "shard", 1).astype(weights_a.dtype),
        passed_along(weights_b.astype(jnp.bfloat16), "shard", 1).astype(weights_b.dtype),
    )
    return (moved_a[None], moved_b[None], own_errors.astype(jnp.bfloat16)[None])


def solution(mesh):
    in_specs = (
        P("shard", "batch", None),
        P("shard", "batch", None),
        P(None, "shard", "batch"),
        P("shard", None, "batch"),
        P("shard", "batch", None),
        P(None, "shard", None, "batch"),
        P(None, "shard", "batch", None),
    )
    out_specs = (P("shard", None, "batch"), P("shard", "batch", None), P("shard", "batch", None))
    return jax.shard_map(
        per_device, mesh=mesh, in_specs=in_specs, out_specs=out_specs, check_vma=False
    )
```

profile of v0, /device:TPU:0, one launch (start us, length us, event | category | flops | bytes accessed | tf_op | source)
XLA Modules:
  0.0 173.4 jit_solution(172406984584624309)
XLA Ops:
  7.2 0.7 compare_and_fusion
  7.9 0.1 copy-done
  8.1 0.9 gather_fusion
  8.9 0.8 broadcast_select_fusion.1
  9.8 0.0 reduce-scatter.3.cloned.1.call-start
  9.8 30.0 %all-gather.3.cloned.1.call-done = bf16[512,1024]{1,0:T(8,128)(2,1)} async-done(((bf16[128,1024]{1,0:T(8,128)(2,1)}), bf16[512,1024]{1,0:T(8,128)(2,1)}) %all-gather.3.cloned.1.call-update) | async-done | bytes 1048592 | tf_op jit(solution)/shard_map/all_gather | solution.py:35
  39.8 2.6 %fusion.13 = f32[512,512]{1,0:T(8,128)S(1)} fusion(bf16[512,1024]{1,0:T(8,128)(2,1)} %all-gather.3.cloned.1.call-done, f32[1,1024,512]{2,1,0:T(8,128)} %param.14), kind=kOutput, calls=%fused_computation.30 | convolution fusion | flops 537133056 | bytes 4194304 | tf_op jit(solution)/shard_map/dot_general | solution.py:36
  42.4 1.2 fusion.17
  43.7 0.0 all-gather.5.cloned.1.call-start
  43.8 0.9 gather_fusion.2
  44.6 0.8 broadcast_select_fusion
  45.5 0.0 reduce-scatter.5.cloned.1.call-start
  45.5 0.8 gather_fusion.1
  46.4 22.3 %reduce-scatter.3.cloned.1.call-done = bf16[128,512]{1,0:T(8,128)(2,1)} async-done(((bf16[512,512]{1,0:T(8,128)(2,1)}), bf16[128,512]{1,0:T(8,128)(2,1)}) %reduce-scatter.3.cloned.1.call-update) | async-done | bytes 131088 | tf_op jit(solution)/shard_map/reduce_scatter | solution.py:38
  68.6 1.0 multiply_convert_fusion.1
  69.7 10.0 %all_gather.13 = bf16[512,512]{1,0:T(8,128)(2,1)S(1)} all-gather(bf16[128,512]{1,0:T(8,128)(2,1)S(1)} %multiply_convert_fusion.1), channel_id=1, replica_groups=mesh['shard'=8,'batch'=4] {'batch'}, dimensions={0}, use_global_device_ids=true | all-gather | bytes 655360 | tf_op jit(solution)/shard_map/all_gather | solution.py:47
  79.7 0.8 copy-done.3
  80.5 1.6 fusion.10
  82.1 5.0 %bitcast_add_fusion.1 = f32[1024,512]{1,0:T(8,128)} fusion(f32[1,1024,512]{2,1,0:T(8,128)} %param.14, bf16[512,1024]{1,0:T(8,128)(2,1)} %all-gather.3.cloned.1.call-done, bf16[512,512]{1,0:T(8,128)(2,1)} %copy-done.3, bf16[2,1,1024,512]{3,2,1,0:T(8,128)(2,1)} %param.16, f32[512,512]{1,0:T(8,128)S(1)} %fusion.13, f32[1,512,512]{2,1,0:T(8,128)S(1)} %copy-done.2), kind=kOutput, calls=%fused_computation.6 | convolution fusion | flops 810287104 | bytes 8912896 | tf_op jit(solution)/shard_map/dot_general | solution.py:60
  87.1 10.2 %all-gather.5.cloned.1.call-done = bf16[512,1024]{1,0:T(8,128)(2,1)} async-done(((bf16[128,1024]{1,0:T(8,128)(2,1)}), bf16[512,1024]{1,0:T(8,128)(2,1)}) %all-gather.5.cloned.1.call-update) | async-done | bytes 1048592 | tf_op jit(solution)/shard_map/all_gather | solution.py:35
  97.3 2.6 %fusion.11 = f32[512,512]{1,0:T(8,128)S(1)} fusion(bf16[512,1024]{1,0:T(8,128)(2,1)} %all-gather.5.cloned.1.call-done, f32[1024,512]{1,0:T(8,128)} %bitcast_add_fusion.1), kind=kOutput, calls=%fused_computation.25 | convolution fusion | flops 537657344 | bytes 4194304 | tf_op jit(solution)/shard_map/dot_general | solution.py:36
  99.9 1.2 fusion.18
  101.2 0.8 gather_fusion.3
  102.1 24.1 %reduce-scatter.5.cloned.1.call-done = bf16[128,512]{1,0:T(8,128)(2,1)} async-done(((bf16[512,512]{1,0:T(8,128)(2,1)}), bf16[128,512]{1,0:T(8,128)(2,1)}) %reduce-scatter.5.cloned.1.call-update) | async-done | bytes 131088 | tf_op jit(solution)/shard_map/reduce_scatter | solution.py:38
  126.2 1.7 fusion.36
  127.8 9.9 %all_gather.15 = bf16[512,512]{1,0:T(8,128)(2,1)S(1)} all-gather(bf16[128,512]{1,0:T(8,128)(2,1)S(1)} %get-tuple-element.10), channel_id=1, replica_groups=mesh['shard'=8,'batch'=4] {'batch'}, dimensions={0}, use_global_device_ids=true | all-gather | bytes 655360 | tf_op jit(solution)/shard_map/all_gather | solution.py:47
  137.8 4.5 %fusion = bf16[1024,512]{1,0:T(8,128)(2,1)} fusion(f32[1024,512]{1,0:T(8,128)} %bitcast_add_fusion.1, bf16[512,1024]{1,0:T(8,128)(2,1)} %all-gather.5.cloned.1.call-done, bf16[512,512]{1,0:T(8,128)(2,1)S(1)} %all_gather.15, bf16[2,1,1024,512]{3,2,1,0:T(8,128)(2,1)} %param.16, f32[512,512]{1,0:T(8,128)S(1)} %fusion.11, f32[512,512]{1,0:T(8,128)S(1)} %fusion.10), kind=kOutput, calls=%fused_computation.5 | convolution fusion | flops 811073536 | bytes 7864320 | tf_op jit(solution)/shard_map/dot_general | solution.py:60
  142.3 1.6 fusion.16
  144.0 1.7 collective-permute-start.1
  145.6 18.6 %collective-permute-done.1 = bf16[512,512]{1,0:T(8,128)(2,1)S(1)} collective-permute-done((bf16[512,512]{1,0:T(8,128)(2,1)S(1)}, bf16[512,512]{1,0:T(8,128)(2,1)S(1)}, u32[]{:S(2)}, u32[]{:S(2)}) %collective-permute-start.1) | collective-permute-done | bytes 524320 | tf_op jit(solution)/shard_map/ppermute | solution.py:18
  164.2 1.1 bitcast_convert_fusion.4
  165.3 1.6 bitcast_convert_fusion.2
  (15 shorter events, 0.1 us)
Async XLA Ops:
  7.2 0.9 copy-start
  7.2 32.6 %all-gather.3.cloned.1.call-start = ((), (), s32[]{:S(2)}) async-start(), calls=%async_computation.2 | async-start | bytes 1310720 | tf_op jit(solution)/shard_map/all_gather | solution.py:35
  9.8 32.7 %copy-start.2 = (f32[1,512,512]{2,1,0:T(8,128)S(1)}, f32[1,512,512]{2,1,0:T(8,128)}, u32[]{:S(2)}) copy-start(f32[1,512,512]{2,1,0:T(8,128)} %param.15) | copy-start | bytes 3145732
  9.8 58.9 %reduce-scatter.3.cloned.1.call-start = ((), (), s32[]{:S(2)}) async-start(), calls=%async_computation.3 | async-start | bytes 655360 | tf_op jit(solution)/shard_map/reduce_scatter | solution.py:38
  43.7 1.8 %copy-start.1 = (bf16[1,64,512]{2,1,0:T(8,128)(2,1)S(1)}, bf16[1,64,512]{2,1,0:T(8,128)(2,1)}, u32[]{:S(2)}) copy-start(bf16[1,64,512]{2,1,0:T(8,128)(2,1)} %param.12) | copy-start | bytes 196612
  43.7 53.6 %all-gather.5.cloned.1.call-start = ((), (), s32[]{:S(2)}) async-start(), calls=%async_computation.4 | async-start | bytes 1310720 | tf_op jit(solution)/shard_map/all_gather | solution.py:35
  45.5 80.7 %reduce-scatter.5.cloned.1.call-start = ((), (), s32[]{:S(2)}) async-start(), calls=%async_computation.5 | async-start | bytes 655360 | tf_op jit(solution)/shard_map/reduce_scatter | solution.py:38
  79.7 0.8 copy-start.3
  142.3 23.0 %collective-permute-start = (bf16[1024,512]{1,0:T(8,128)(2,1)}, bf16[1024,512]{1,0:T(8,128)(2,1)S(1)}, u32[]{:S(2)}, u32[]{:S(2)}) collective-permute-start(bf16[1024,512]{1,0:T(8,128)(2,1)} %fusion), channel_id=1, source_target_pairs={{0,4},{4,8},{8,12},{12,16},{16,20},{20,24},{24,28},{28,0},{1,5},{5... | collective-permute-start | bytes 3145736 | tf_op jit(solution)/shard_map/ppermute | solution.py:18
  144.0 20.2 %collective-permute-start.1 = (bf16[512,512]{1,0:T(8,128)(2,1)S(1)}, bf16[512,512]{1,0:T(8,128)(2,1)S(1)}, u32[]{:S(2)}, u32[]{:S(2)}) collective-permute-start(bf16[512,512]{1,0:T(8,128)(2,1)S(1)} %fusion.16), channel_id=1, source_target_pairs={{0,4},{4,8},{8,12},{12,16},{16,20},{20,24},{24,28},{28,0},{1,5},{5... | collective-permute-start | bytes 1572872 | tf_op jit(solution)/shard_map/ppermute | solution.py:18
Sparse Core Ops, SparseCore 0:
  10.4 29.3 all-gather.2
  43.8 24.7 reduce-scatter.2
  70.6 26.6 all-gather.4
  101.3 24.7 reduce-scatter.4
where the time goes:
time: 174 us; the launch traced here: 173 us
  waiting for transfers between devices  105 us (60%)
  matrix products  20.5 us (12%)
  blocking collectives  20 us (11%)
  between operations  13.9 us (8%)
  other arithmetic  7.74 us (4%)
  local copies, waits for them, and re-layouts  4.36 us (3%)
  starting transfers between devices  1.82 us (1%)
    reduce_scatter x2, waiting for transfers between devices, per_device(): lax.psum_scatter((jnp.dot(hidden_b, bf_b, preferred_element_type=jnp.floa...  46.4 us
    all_gather x2, waiting for transfers between devices, per_device(): all_rows = lax.all_gather(local_rows, 'batch', axis=0, tiled=True)  40.2 us
    all_gather x2, blocking collectives, per_device(): lax.all_gather((precision_obs * own_errors).astype(jnp.bfloat16), 'batch'...  20 us
    ppermute x2, waiting for transfers between devices, passed_along(): lax.ppermute(value, axis, [(i, (i + by) % size) for i in range(size)])  18.6 us
    dot_general x2, matrix products, per_device(): lax.dot_general(all_rows, back_hidden, contract_rows, preferred_element_t...  9.51 us
    dot_general x2, matrix products, per_device(): jnp.dot(all_rows, bf_a, preferred_element_type=jnp.float32) * scale_in  5.27 us
    broadcast_in_dim x3, other arithmetic, per_device(): return (moved_a[None], moved_b[None], own_errors.astype(jnp.bfloat16)[None])  4.4 us
  transfers between devices with their start and end apart: 6, of which 5 were waited for; matrix products, arithmetic and copies ran while one was open for 8% of the time, Pallas kernels for 0%

commit v1 on v0

v1 whole, which is shorter than its diff:
```python
import functools

import jax
import jax.numpy as jnp
from jax import lax
from jax.experimental import pallas as pl
from jax.experimental.pallas import tpu as pltpu
from jax.sharding import PartitionSpec as P

D_IN = 1024
HID = 2048
STEPS = 2
half_step = 0.01
keep = 1.0 - half_step
root_step = 0.02**0.5
precision_obs = 32.0
scale_in = D_IN ** (-0.5)
scale_hid = HID ** (-0.5)
MESH = pl.DeviceIdType.MESH
TN = (((0,), (0,)), ((), ()))
NT = (((1,), (1,)), ((), ()))
f32 = jnp.float32
bf16 = jnp.bfloat16


def kernel(
    ns, nb, x_in, t_in, picks, l1, l2, n1h, n2h,
    d_out, x_out, c_out, m2_out, errs,
    x, w1, w2, n1, n2, w1b, w2b, h, hb, bh0, dsend, csend, m2send, share, share_in, sw,
    load_sem, xs_sem, xr_sem, ss_sem, sr_sem, gs_sem, gr_sem, hs_sem, hr_sem,
):
    s = lax.axis_index("shard")
    b = lax.axis_index("batch")
    nxt = (lax.rem(s + 1, ns), b)
    prv = (lax.rem(s + ns - 1, ns), b)
    rows = x_in.shape[0]

    loads = [
        pltpu.make_async_copy(src, dst, load_sem.at[i])
        for i, (src, dst) in enumerate(((l1, w1), (n1h, n1), (l2, w2), (n2h, n2)))
    ]
    for load in loads:
        load.start()

    barrier = pltpu.get_barrier_semaphore()
    peers = [(s, lax.rem(b + k, nb)) for k in range(nb)]
    owners = [(s, lax.rem(b + nb - k, nb)) for k in range(nb)]
    for who in peers[1:] + [nxt, prv]:
        pl.semaphore_signal(barrier, inc=1, device_id=who, device_id_type=MESH)
    pl.semaphore_wait(barrier, nb + 1)

    sends = []

    def remote(src, dst, send, recv, who):
        copy = pltpu.make_async_remote_copy(
            src_ref=src, dst_ref=dst, send_sem=send, recv_sem=recv,
            device_id=who, device_id_type=MESH,
        )
        copy.start()
        sends.append(copy)
        return copy

    def slot(k):
        return pl.ds(k * rows, rows)

    gathers = [
        remote(x_in, x.at[slot(k)], xs_sem.at[k], xr_sem.at[k], peers[k])
        for k in range(1, nb)
    ]
    x[slot(0), :] = x_in[...]

    loads[0].wait()
    loads[1].wait()
    hops = []
    quarter = D_IN // 4
    for q in range(4):
        @pl.loop(0, quarter, step=32)
        def _(r, q=q):
            part = pl.ds(q * quarter + r, 32)
            w = w1[part, :]
            w1b[part, :] = w.astype(bf16)
            w = keep * w + root_step * n1[0, part, :].astype(f32)
            w1[part, :] = w
            dsend[part, :] = (keep * w + root_step * n1[1, part, :].astype(f32)).astype(bf16)
        piece = pl.ds(q * quarter, quarter)
        hops.append(remote(dsend.at[piece], d_out.at[piece], hs_sem.at[q], hr_sem.at[q], nxt))
    loads[2].wait()
    loads[3].wait()
    for copy in gathers:
        copy.wait_recv()
    hops.append(remote(x, x_out, hs_sem.at[4], hr_sem.at[4], nxt))

    for step in range(STEPS):
        w2b[...] = w2[...].astype(bf16)
        hidden = jnp.tanh(jnp.dot(x[...], w1b[...], preferred_element_type=f32) * scale_in)
        h[...] = hidden
        hb[...] = hidden.astype(bf16)
        share[step] = (
            jnp.dot(hb[...], w2b[...], preferred_element_type=f32) * scale_hid
        ).astype(bf16)
        scatters = [
            remote(
                share.at[step, slot(k)], share_in.at[step, k],
                ss_sem.at[step, k], sr_sem.at[step, k], owners[k],
            )
            for k in range(1, nb)
        ]
        @pl.loop(0, w2.shape[0], step=32)
        def _(r):
            part = pl.ds(r, 32)
            w2[part, :] = keep * w2[part, :] + root_step * n2[step, part, :].astype(f32)

        picked = lax.broadcasted_iota(jnp.int32, (rows, picks.shape[2]), 0) == picks[step]
        picked = jnp.where(picked, 1.0, 0.0)
        counts = jnp.sum(picked, axis=1, keepdims=True)
        predicted = share[step, slot(0), :].astype(f32)
        for k in range(1, nb):
            scatters[k - 1].wait_recv()
            predicted = predicted + share_in[step, k].astype(f32)
        errors = predicted - t_in[...].astype(f32)
        signal = (precision_obs * errors).astype(bf16).astype(f32)
        sw[step, slot(0), :] = (counts * signal).astype(bf16)
        signals = [
            remote(
                sw.at[step, slot(0)], sw.at[step, slot(k)],
                gs_sem.at[step, k], gr_sem.at[step, k], peers[k],
            )
            for k in range(1, nb)
        ]
        if step == STEPS - 1:
            errs[...] = lax.dot_general(
                picked.astype(bf16), errors.astype(bf16), TN, preferred_element_type=f32
            ).astype(bf16)
        for copy in signals:
            copy.wait_recv()
        back = (
            lax.dot_general(sw[step], w2b[...], NT, preferred_element_type=f32)
            * scale_hid
            * (1.0 - h[...] * h[...])
        )
        if step == 0:
            bh0[...] = back.astype(bf16)
        else:
            csend[...] = (keep * bh0[...].astype(f32) + back).astype(bf16)
            hops.append(remote(csend, c_out, hs_sem.at[5], hr_sem.at[5], nxt))
        grad_two = lax.dot_general(hb[...], sw[step], TN, preferred_element_type=f32)
        final_two = w2[...] - (half_step * scale_hid) * grad_two
        if step == 0:
            w2[...] = final_two
            for q in range(4):
                piece = pl.ds(q * quarter, quarter)
                grad_one = lax.dot_general(x[:, piece], bh0[...], TN, preferred_element_type=f32)
                w1b[piece, :] = (w1[piece, :] - (half_step * scale_in) * grad_one).astype(bf16)
        else:
            m2send[...] = final_two.astype(bf16)
            hops.append(remote(m2send, m2_out, hs_sem.at[6], hr_sem.at[6], nxt))
    for copy in hops:
        copy.wait_recv()
    for copy in sends:
        copy.wait_send()


def per_device(ns, nb, data_inputs, data_targets, row_picks, layer_one, layer_two, noise_one, noise_two):
    x_in, t_in, l1, l2 = data_inputs[0], data_targets[0], layer_one[0], layer_two[0]
    n1h, n2h = noise_one[:, 0], noise_two[:, 0]
    rows, d_in = x_in.shape
    d_out = t_in.shape[1]
    hid = l1.shape[1]
    total = rows * nb
    mine = row_picks.shape[2]
    any_spec = pl.BlockSpec(memory_space=pl.ANY)
    vmem = pl.BlockSpec(memory_space=pltpu.VMEM)
    V = pltpu.VMEM
    D = pltpu.SemaphoreType.DMA
    dd, xx, cc, m2, errs = pl.pallas_call(
        functools.partial(kernel, ns, nb),
        out_shape=(
            jax.ShapeDtypeStruct((d_in, hid), bf16),
            jax.ShapeDtypeStruct((total, d_in), bf16),
            jax.ShapeDtypeStruct((total, hid), bf16),
            jax.ShapeDtypeStruct((hid, d_out), bf16),
            jax.ShapeDtypeStruct((mine, d_out), bf16),
        ),
        in_specs=[vmem] * 3 + [any_spec] * 4,
        out_specs=(any_spec,) * 4 + (vmem,),
        scratch_shapes=[
            V((total, d_in), bf16),
            V((d_in, hid), f32),
            V((hid, d_out), f32),
            V((STEPS, d_in, hid), bf16),
            V((STEPS, hid, d_out), bf16),
            V((d_in, hid), bf16),
            V((hid, d_out), bf16),
            V((total, hid), f32),
            V((total, hid), bf16),
            V((total, hid), bf16),
            V((d_in, hid), bf16),
            V((total, hid), bf16),
            V((hid, d_out), bf16),
            V((STEPS, total, d_out), bf16),
            V((STEPS, nb, rows, d_out), bf16),
            V((STEPS, total, d_out), bf16),
            D((4,)), D((nb,)), D((nb,)),
            D((STEPS, nb)), D((STEPS, nb)), D((STEPS, nb)), D((STEPS, nb)),
            D((7,)), D((7,)),
        ],
        compiler_params=pltpu.CompilerParams(
            collective_id=0, has_side_effects=True, vmem_limit_bytes=40 * 1024 * 1024
        ),
    )(x_in, t_in, row_picks, l1, l2, n1h, n2h)
    grad = lax.dot_general(xx, cc, TN, preferred_element_type=f32)
    moved_a = dd.astype(f32) - (half_step * scale_in) * grad
    return moved_a[None], m2.astype(f32)[None], errs[None]


def solution(mesh):
    in_specs = (
        P("shard", "batch", None),
        P("shard", "batch", None),
        P(None, "shard", "batch"),
        P("shard", None, "batch"),
        P("shard", "batch", None),
        P(None, "shard", None, "batch"),
        P(None, "shard", "batch", None),
    )
    out_specs = (P("shard", None, "batch"), P("shard", "batch", None), P("shard", "batch", None))
    return jax.shard_map(
        functools.partial(per_device, mesh.shape["shard"], mesh.shape["batch"]),
        mesh=mesh, in_specs=in_specs, out_specs=out_specs, check_vma=False,
    )
```

time: 174 us -> 54.4 us (0.31)
  waiting for transfers between devices: 105 us -> 0 us
  Pallas kernels: 0 us -> 41.8 us
  blocking collectives: 20 us -> 0 us
  matrix products: 20.5 us -> 1.79 us
  between operations: 13.9 us -> 0.66 us
  other arithmetic: 7.74 us -> 1.1 us
  local copies, waits for them, and re-layouts: 4.36 us -> 8.7 us
  starting transfers between devices: 1.82 us -> 0 us
    reduce_scatter x2 -> x0, waiting for transfers between devices: 46.4 us -> none  [per_device(): lax.psum_scatter((jnp.dot(hidden_b, bf_b, preferred_element_type=jnp.floa...]
    pallas_call x0 -> x1, Pallas kernels: none -> 41.8 us  [per_device(): pl.pallas_call(functools.partial(kernel, ns, nb), out_shape=(jax.ShapeDty...]
    all_gather x2 -> x0, waiting for transfers between devices: 40.2 us -> none  [per_device(): all_rows = lax.all_gather(local_rows, 'batch', axis=0, tiled=True)]
    all_gather x2 -> x0, blocking collectives: 20 us -> none  [per_device(): lax.all_gather((precision_obs * own_errors).astype(jnp.bfloat16), 'batch'...]
    dot_general x8 -> x1, matrix products: 20.5 us -> 1.79 us  [per_device(): grad = lax.dot_general(xx, cc, TN, preferred_element_type=f32)]
    ppermute x2 -> x0, waiting for transfers between devices: 18.6 us -> none  [passed_along(): lax.ppermute(value, axis, [(i, (i + by) % size) for i in range(size)])]
    unnamed x8 -> x15, local copies, waits for them, and re-layouts: 0.94 us -> 8.7 us
    gather x4 -> x0, local copies, waits for them, and re-layouts: 3.42 us -> none  [the longest x2 1.72 us: per_device(): local_rows = jnp.take(data_inputs[0], chosen, axis=0)]
  transfers between devices with their start and end apart: 6 -> 0, of which waited for: 5 -> 0; matrix products, arithmetic and copies ran while one was open for 8% -> 0% of each run, Pallas kernels for 0% -> 0%
where the time goes in v1:
time: 54.4 us; the launch traced here: 54.1 us
  Pallas kernels  41.8 us (77%)
  local copies, waits for them, and re-layouts  8.7 us (16%)
  matrix products  1.79 us (3%)
  other arithmetic  1.1 us (2%)
  between operations  0.66 us (1%)
    pallas_call x1, Pallas kernels, per_device(): pl.pallas_call(functools.partial(kernel, ns, nb), out_shape=(jax.ShapeDty...  41.8 us
    unnamed x15, local copies, waits for them, and re-layouts  8.7 us
    dot_general x1, matrix products, per_device(): grad = lax.dot_general(xx, cc, TN, preferred_element_type=f32)  1.79 us
    broadcast_in_dim x1, other arithmetic, per_device(): return (moved_a[None], m2.astype(f32)[None], errs[None])  1.1 us

profile of v1, /device:TPU:0, one launch (start us, length us, event | category | flops | bytes accessed | tf_op | source)
XLA Modules:
  0.0 54.1 jit_solution(957727832460195917)
XLA Ops:
  0.6 0.0 copy-start
  0.6 1.6 %copy-done = f32[1,1024,512]{2,1,0:T(8,128)S(1)} copy-done((f32[1,1024,512]{2,1,0:T(8,128)S(1)}, f32[1,1024,512]{2,1,0:T(8,128)}, u32[]{:S(2)}) %copy-start) | copy-done | bytes 2097176
  2.2 0.0 copy-start.1
  2.2 1.6 %copy-done.1 = bf16[2,1,1024,512]{3,2,1,0:T(8,128)(2,1)S(1)} copy-done((bf16[2,1,1024,512]{3,2,1,0:T(8,128)(2,1)S(1)}, bf16[2,1,1024,512]{3,2,1,0:T(8,128)(2,1)}, u32[]{:S(2)}) %copy-start.1) | copy-done | bytes 2097176
  3.8 0.0 copy-start.2
  3.8 1.2 %copy-done.2 = f32[1,512,512]{2,1,0:T(8,128)S(1)} copy-done((f32[1,512,512]{2,1,0:T(8,128)S(1)}, f32[1,512,512]{2,1,0:T(8,128)}, u32[]{:S(2)}) %copy-start.2) | copy-done | bytes 1048600
  5.0 0.0 copy-start.3
  5.0 1.2 %copy-done.3 = bf16[2,1,512,512]{3,2,1,0:T(8,128)(2,1)S(1)} copy-done((bf16[2,1,512,512]{3,2,1,0:T(8,128)(2,1)S(1)}, bf16[2,1,512,512]{3,2,1,0:T(8,128)(2,1)}, u32[]{:S(2)}) %copy-start.3) | copy-done | bytes 1048600
  6.3 0.0 copy-start.4
  6.3 0.9 %copy-done.4 = bf16[1,64,1024]{2,1,0:T(8,128)(2,1)S(1)} copy-done((bf16[1,64,1024]{2,1,0:T(8,128)(2,1)S(1)}, bf16[1,64,1024]{2,1,0:T(8,128)(2,1)}, u32[]{:S(2)}) %copy-start.4) | copy-done | bytes 131096
  7.2 0.0 copy-start.5
  7.2 0.8 %copy-done.5 = bf16[1,64,512]{2,1,0:T(8,128)(2,1)S(1)} copy-done((bf16[1,64,512]{2,1,0:T(8,128)(2,1)S(1)}, bf16[1,64,512]{2,1,0:T(8,128)(2,1)}, u32[]{:S(2)}) %copy-start.5) | copy-done | bytes 65560
  8.0 0.0 copy-start.6
  8.0 0.7 %copy-done.6 = s32[2,1,128]{2,1,0:T(1,128)S(1)} copy-done((s32[2,1,128]{2,1,0:T(1,128)S(1)}, s32[2,1,128]{2,1,0:T(1,128)}, u32[]{:S(2)}) %copy-start.6) | copy-done | bytes 1048
  8.7 41.8 %shard_map.94 = (bf16[1024,512]{1,0:T(8,128)(2,1)S(1)}, bf16[256,1024]{1,0:T(8,128)(2,1)S(1)}, bf16[256,512]{1,0:T(8,128)(2,1)S(1)}, bf16[512,512]{1,0:T(8,128)(2,1)S(1)}, bf16[128,512]{1,0:T(8,128)(2,1)S(1)}) custom-call(bf16[64,1024]{1,0:T(8,128)(2,1)S(1)} %bitcast.18, bf16[64,512]{1,0:T(8,128)(2,1)S(1)} %bitcast.20, s32[2,1,128]{2,1,0:T(1,128)S(1)} %copy-done.6, ...), custom_call_target="tpu_custom_call" | custom-call | tf_op jit(solution)/shard_map/pallas_call | solution.py:175
  50.5 1.8 %subtract_bitcast_fusion = f32[1,1024,512]{2,1,0:T(8,128)} fusion(bf16[1024,512]{1,0:T(8,128)(2,1)S(1)} %get-tuple-element.8, bf16[256,1024]{1,0:T(8,128)(2,1)S(1)} %get-tuple-element.9, bf16[256,512]{1,0:T(8,128)(2,1)S(1)} %get-tuple-element.10), kind=kOutput, calls=%fused_computation | convolution fusion | flops 270008320 | bytes 3932160 | tf_op jit(solution)/shard_map/dot_general | solution.py:211
  52.3 1.1 %bitcast_convert_fusion = f32[1,512,512]{2,1,0:T(8,128)} fusion(bf16[512,512]{1,0:T(8,128)(2,1)S(1)} %get-tuple-element.11), kind=kLoop, calls=%fused_computation.1 | loop fusion | flops 262144 | bytes 1572864 | tf_op jit(solution)/shard_map/broadcast_in_dim | solution.py:213
  53.4 0.7 %copy.11 = bf16[1,128,512]{2,1,0:T(8,128)(2,1)} copy(bf16[1,128,512]{2,1,0:T(8,128)(2,1)S(1)} %bitcast.19) | data formatting | bytes 262144
Async XLA Ops:
  0.6 1.6 %copy-start = (f32[1,1024,512]{2,1,0:T(8,128)S(1)}, f32[1,1024,512]{2,1,0:T(8,128)}, u32[]{:S(2)}) copy-start(f32[1,1024,512]{2,1,0:T(8,128)} %param.10) | copy-start | bytes 6291460
  2.2 1.6 %copy-start.1 = (bf16[2,1,1024,512]{3,2,1,0:T(8,128)(2,1)S(1)}, bf16[2,1,1024,512]{3,2,1,0:T(8,128)(2,1)}, u32[]{:S(2)}) copy-start(bf16[2,1,1024,512]{3,2,1,0:T(8,128)(2,1)} %param.12) | copy-start | bytes 6291460
  3.8 1.2 %copy-start.2 = (f32[1,512,512]{2,1,0:T(8,128)S(1)}, f32[1,512,512]{2,1,0:T(8,128)}, u32[]{:S(2)}) copy-start(f32[1,512,512]{2,1,0:T(8,128)} %param.11) | copy-start | bytes 3145732
  5.0 1.2 %copy-start.3 = (bf16[2,1,512,512]{3,2,1,0:T(8,128)(2,1)S(1)}, bf16[2,1,512,512]{3,2,1,0:T(8,128)(2,1)}, u32[]{:S(2)}) copy-start(bf16[2,1,512,512]{3,2,1,0:T(8,128)(2,1)} %param.13) | copy-start | bytes 3145732
  6.3 0.9 %copy-start.4 = (bf16[1,64,1024]{2,1,0:T(8,128)(2,1)S(1)}, bf16[1,64,1024]{2,1,0:T(8,128)(2,1)}, u32[]{:S(2)}) copy-start(bf16[1,64,1024]{2,1,0:T(8,128)(2,1)} %param.7) | copy-start | bytes 393220
  7.2 0.8 %copy-start.5 = (bf16[1,64,512]{2,1,0:T(8,128)(2,1)S(1)}, bf16[1,64,512]{2,1,0:T(8,128)(2,1)}, u32[]{:S(2)}) copy-start(bf16[1,64,512]{2,1,0:T(8,128)(2,1)} %param.8) | copy-start | bytes 196612
  8.0 0.7 %copy-start.6 = (s32[2,1,128]{2,1,0:T(1,128)S(1)}, s32[2,1,128]{2,1,0:T(1,128)}, u32[]{:S(2)}) copy-start(s32[2,1,128]{2,1,0:T(1,128)} %picks.1) | copy-start | bytes 3076

commit v2 on v1

--- a/solution.py
+++ b/solution.py
@@ -27,7 +27,7 @@
     ns, nb, x_in, t_in, picks, l1, l2, n1h, n2h,
     d_out, x_out, c_out, m2_out, errs,
     x, w1, w2, n1, n2, w1b, w2b, h, hb, bh0, dsend, csend, m2send, share, share_in, sw,
-    load_sem, xs_sem, xr_sem, ss_sem, sr_sem, gs_sem, gr_sem, hs_sem, hr_sem,
+    load_sem, xs_sem, xr_sem, ss_sem, sr_sem, gs_sem, gr_sem, hs_sem, hr_sem, fs_sem, fr_sem,
 ):
     s = lax.axis_index("shard")
     b = lax.axis_index("batch")
@@ -67,6 +67,7 @@
         remote(x_in, x.at[slot(k)], xs_sem.at[k], xr_sem.at[k], peers[k])
         for k in range(1, nb)
     ]
+    passed = remote(x_in, x_out.at[slot(0)], hs_sem.at[4], hr_sem.at[4], nxt)
     x[slot(0), :] = x_in[...]
 
     loads[0].wait()
@@ -88,7 +89,6 @@
     loads[3].wait()
     for copy in gathers:
         copy.wait_recv()
-    hops.append(remote(x, x_out, hs_sem.at[4], hr_sem.at[4], nxt))
 
     for step in range(STEPS):
         w2b[...] = w2[...].astype(bf16)
@@ -105,6 +105,13 @@
             )
             for k in range(1, nb)
         ]
+        if step == 0:
+            passed.wait_recv()
+            hops += [
+                remote(x_out.at[slot(0)], x_out.at[slot(k)], fs_sem.at[k], fr_sem.at[k], peers[k])
+                for k in range(1, nb)
+            ]
+
         @pl.loop(0, w2.shape[0], step=32)
         def _(r):
             part = pl.ds(r, 32)
@@ -202,10 +209,10 @@
             V((STEPS, total, d_out), bf16),
             D((4,)), D((nb,)), D((nb,)),
             D((STEPS, nb)), D((STEPS, nb)), D((STEPS, nb)), D((STEPS, nb)),
-            D((7,)), D((7,)),
+            D((7,)), D((7,)), D((nb,)), D((nb,)),
         ],
         compiler_params=pltpu.CompilerParams(
-            collective_id=0, has_side_effects=True, vmem_limit_bytes=40 * 1024 * 1024
+            collective_id=0, has_side_effects=True, vmem_limit_bytes=60 * 1024 * 1024
         ),
     )(x_in, t_in, row_picks, l1, l2, n1h, n2h)
     grad = lax.dot_general(xx, cc, TN, preferred_element_type=f32)

time: 54.4 us -> 55 us (1.011)
  local copies, waits for them, and re-layouts: 8.7 us -> 0.66 us
  Pallas kernels: 41.8 us -> 49.1 us
  matrix products: 1.79 us -> 3.32 us
    unnamed x15 -> x5, local copies, waits for them, and re-layouts: 8.7 us -> 0.66 us
    pallas_call x1, Pallas kernels: 41.8 us -> 49.1 us  [per_device(): pl.pallas_call(functools.partial(kernel, ns, nb), out_shape=(jax.ShapeDty...]
    dot_general x1, matrix products: 1.79 us -> 3.32 us  [per_device(): grad = lax.dot_general(xx, cc, TN, preferred_element_type=f32)]
where the time goes in v2:
time: 55 us; the launch traced here: 54.8 us
  Pallas kernels  49.1 us (89%)
  matrix products  3.32 us (6%)
  other arithmetic  1.1 us (2%)
  local copies, waits for them, and re-layouts  0.66 us (1%)
  between operations  0.66 us (1%)
    pallas_call x1, Pallas kernels, per_device(): pl.pallas_call(functools.partial(kernel, ns, nb), out_shape=(jax.ShapeDty...  49.1 us
    dot_general x1, matrix products, per_device(): grad = lax.dot_general(xx, cc, TN, preferred_element_type=f32)  3.32 us
    broadcast_in_dim x1, other arithmetic, per_device(): return (moved_a[None], m2.astype(f32)[None], errs[None])  1.1 us

profile of v2, /device:TPU:0, one launch (start us, length us, event | category | flops | bytes accessed | tf_op | source)
XLA Modules:
  0.0 54.8 jit_solution(17050780132592801179)
XLA Ops:
  0.6 49.1 %shard_map.94 = (bf16[1024,512]{1,0:T(8,128)(2,1)}, bf16[256,1024]{1,0:T(8,128)(2,1)}, bf16[256,512]{1,0:T(8,128)(2,1)}, bf16[512,512]{1,0:T(8,128)(2,1)}, bf16[128,512]{1,0:T(8,128)(2,1)}) custom-call(bf16[64,1024]{1,0:T(8,128)(2,1)} %bitcast.18, bf16[64,512]{1,0:T(8,128)(2,1)} %bitcast.20, s32[2,1,128]{2,1,0:T(1,128)} %picks.1, f32[1024,512]{1,0:T(8,128)} %bitcast.14, ...), custom_call_target="tpu_custom_call" | custom-call | tf_op jit(solution)/shard_map/pallas_call | solution.py:182
  49.7 0.0 copy-start
  49.7 0.0 copy-start.1
  49.7 3.3 %subtract_bitcast_fusion = f32[1,1024,512]{2,1,0:T(8,128)} fusion(bf16[1024,512]{1,0:T(8,128)(2,1)} %get-tuple-element.8, bf16[256,1024]{1,0:T(8,128)(2,1)} %get-tuple-element.9, bf16[256,512]{1,0:T(8,128)(2,1)} %get-tuple-element.10), kind=kOutput, calls=%fused_computation | convolution fusion | flops 270008320 | bytes 3932160 | tf_op jit(solution)/shard_map/dot_general | solution.py:218
  53.0 0.0 copy-done
  53.0 1.1 %bitcast_convert_fusion = f32[1,512,512]{2,1,0:T(8,128)} fusion(bf16[512,512]{1,0:T(8,128)(2,1)S(1)} %copy-done), kind=kLoop, calls=%fused_computation.1 | loop fusion | flops 262144 | bytes 1572864 | tf_op jit(solution)/shard_map/broadcast_in_dim | solution.py:220
  54.1 0.0 copy-done.1
  54.1 0.7 %copy.11 = bf16[1,128,512]{2,1,0:T(8,128)(2,1)} copy(bf16[1,128,512]{2,1,0:T(8,128)(2,1)S(1)} %bitcast.19) | data formatting | bytes 262144
Async XLA Ops:
  49.7 3.3 %copy-start = (bf16[512,512]{1,0:T(8,128)(2,1)S(1)}, bf16[512,512]{1,0:T(8,128)(2,1)}, u32[]{:S(2)}) copy-start(bf16[512,512]{1,0:T(8,128)(2,1)} %get-tuple-element.11) | copy-start | bytes 1572868
  49.7 4.4 %copy-start.1 = (bf16[128,512]{1,0:T(8,128)(2,1)S(1)}, bf16[128,512]{1,0:T(8,128)(2,1)}, u32[]{:S(2)}) copy-start(bf16[128,512]{1,0:T(8,128)(2,1)} %get-tuple-element.12) | copy-start | bytes 393220

commit v3 on v2

--- a/solution.py
+++ b/solution.py
@@ -35,9 +35,15 @@
     prv = (lax.rem(s + ns - 1, ns), b)
     rows = x_in.shape[0]
 
+    quarter = D_IN // 4
+    pairs = []
+    for q in range(4):
+        piece = pl.ds(q * quarter, quarter)
+        pairs += [(l1.at[piece], w1.at[piece])]
+        pairs += [(n1h.at[i, piece], n1.at[i, piece]) for i in range(STEPS)]
+    pairs += [(l2, w2)] + [(n2h.at[i], n2.at[i]) for i in range(STEPS)]
     loads = [
-        pltpu.make_async_copy(src, dst, load_sem.at[i])
-        for i, (src, dst) in enumerate(((l1, w1), (n1h, n1), (l2, w2), (n2h, n2)))
+        pltpu.make_async_copy(src, dst, load_sem.at[i]) for i, (src, dst) in enumerate(pairs)
     ]
     for load in loads:
         load.start()
@@ -70,11 +76,11 @@
     passed = remote(x_in, x_out.at[slot(0)], hs_sem.at[4], hr_sem.at[4], nxt)
     x[slot(0), :] = x_in[...]
 
-    loads[0].wait()
-    loads[1].wait()
     hops = []
-    quarter = D_IN // 4
     for q in range(4):
+        for load in loads[3 * q : 3 * q + 3]:
+            load.wait()
+
         @pl.loop(0, quarter, step=32)
         def _(r, q=q):
             part = pl.ds(q * quarter + r, 32)
@@ -85,8 +91,8 @@
             dsend[part, :] = (keep * w + root_step * n1[1, part, :].astype(f32)).astype(bf16)
         piece = pl.ds(q * quarter, quarter)
         hops.append(remote(dsend.at[piece], d_out.at[piece], hs_sem.at[q], hr_sem.at[q], nxt))
-    loads[2].wait()
-    loads[3].wait()
+    for load in loads[12:]:
+        load.wait()
     for copy in gathers:
         copy.wait_recv()
 
@@ -207,7 +213,7 @@
             V((STEPS, total, d_out), bf16),
             V((STEPS, nb, rows, d_out), bf16),
             V((STEPS, total, d_out), bf16),
-            D((4,)), D((nb,)), D((nb,)),
+            D((15,)), D((nb,)), D((nb,)),
             D((STEPS, nb)), D((STEPS, nb)), D((STEPS, nb)), D((STEPS, nb)),
             D((7,)), D((7,)), D((nb,)), D((nb,)),
         ],

time: 55 us -> 55.1 us (level)
  no operation moved by 1% of the time
where the time goes in v3:
time: 55.1 us; the launch traced here: 54.9 us
  Pallas kernels  49.2 us (89%)
  matrix products  3.32 us (6%)
  other arithmetic  1.1 us (2%)
  local copies, waits for them, and re-layouts  0.66 us (1%)
  between operations  0.66 us (1%)
    pallas_call x1, Pallas kernels, per_device(): pl.pallas_call(functools.partial(kernel, ns, nb), out_shape=(jax.ShapeDty...  49.2 us
    dot_general x1, matrix products, per_device(): grad = lax.dot_general(xx, cc, TN, preferred_element_type=f32)  3.32 us
    broadcast_in_dim x1, other arithmetic, per_device(): return (moved_a[None], m2.astype(f32)[None], errs[None])  1.1 us

profile of v3, /device:TPU:0, one launch (start us, length us, event | category | flops | bytes accessed | tf_op | source)
XLA Modules:
  0.0 54.9 jit_solution(17464578521407721892)
XLA Ops:
  0.6 49.2 %shard_map.94 = (bf16[1024,512]{1,0:T(8,128)(2,1)}, bf16[256,1024]{1,0:T(8,128)(2,1)}, bf16[256,512]{1,0:T(8,128)(2,1)}, bf16[512,512]{1,0:T(8,128)(2,1)}, bf16[128,512]{1,0:T(8,128)(2,1)}) custom-call(bf16[64,1024]{1,0:T(8,128)(2,1)} %bitcast.18, bf16[64,512]{1,0:T(8,128)(2,1)} %bitcast.20, s32[2,1,128]{2,1,0:T(1,128)} %picks.1, f32[1024,512]{1,0:T(8,128)} %bitcast.14, ...), custom_call_target="tpu_custom_call" | custom-call | tf_op jit(solution)/shard_map/pallas_call | solution.py:188
  49.8 0.0 copy-start
  49.8 0.0 copy-start.1
  49.8 3.3 %subtract_bitcast_fusion = f32[1,1024,512]{2,1,0:T(8,128)} fusion(bf16[1024,512]{1,0:T(8,128)(2,1)} %get-tuple-element.8, bf16[256,1024]{1,0:T(8,128)(2,1)} %get-tuple-element.9, bf16[256,512]{1,0:T(8,128)(2,1)} %get-tuple-element.10), kind=kOutput, calls=%fused_computation | convolution fusion | flops 270008320 | bytes 3932160 | tf_op jit(solution)/shard_map/dot_general | solution.py:224
  53.1 0.0 copy-done
  53.1 1.1 %bitcast_convert_fusion = f32[1,512,512]{2,1,0:T(8,128)} fusion(bf16[512,512]{1,0:T(8,128)(2,1)S(1)} %copy-done), kind=kLoop, calls=%fused_computation.1 | loop fusion | flops 262144 | bytes 1572864 | tf_op jit(solution)/shard_map/broadcast_in_dim | solution.py:226
  54.2 0.0 copy-done.1
  54.2 0.7 %copy.11 = bf16[1,128,512]{2,1,0:T(8,128)(2,1)} copy(bf16[1,128,512]{2,1,0:T(8,128)(2,1)S(1)} %bitcast.19) | data formatting | bytes 262144
Async XLA Ops:
  49.8 3.3 %copy-start = (bf16[512,512]{1,0:T(8,128)(2,1)S(1)}, bf16[512,512]{1,0:T(8,128)(2,1)}, u32[]{:S(2)}) copy-start(bf16[512,512]{1,0:T(8,128)(2,1)} %get-tuple-element.11) | copy-start | bytes 1572868
  49.8 4.4 %copy-start.1 = (bf16[128,512]{1,0:T(8,128)(2,1)S(1)}, bf16[128,512]{1,0:T(8,128)(2,1)}, u32[]{:S(2)}) copy-start(bf16[128,512]{1,0:T(8,128)(2,1)} %get-tuple-element.12) | copy-start | bytes 393220

commit v4 on v3

--- a/solution.py
+++ b/solution.py
@@ -218,7 +218,7 @@
             D((7,)), D((7,)), D((nb,)), D((nb,)),
         ],
         compiler_params=pltpu.CompilerParams(
-            collective_id=0, has_side_effects=True, vmem_limit_bytes=60 * 1024 * 1024
+            collective_id=0, has_side_effects=True, vmem_limit_bytes=40 * 1024 * 1024
         ),
     )(x_in, t_in, row_picks, l1, l2, n1h, n2h)
     grad = lax.dot_general(xx, cc, TN, preferred_element_type=f32)

time: 55.1 us -> 60.1 us (1.091)
  local copies, waits for them, and re-layouts: 0.66 us -> 8.7 us
  Pallas kernels: 49.2 us -> 47.5 us
  matrix products: 3.32 us -> 1.79 us
    unnamed x5 -> x15, local copies, waits for them, and re-layouts: 0.66 us -> 8.7 us
    pallas_call x1, Pallas kernels: 49.2 us -> 47.5 us  [per_device(): pl.pallas_call(functools.partial(kernel, ns, nb), out_shape=(jax.ShapeDty...]
    dot_general x1, matrix products: 3.32 us -> 1.79 us  [per_device(): grad = lax.dot_general(xx, cc, TN, preferred_element_type=f32)]
where the time goes in v4:
time: 60.1 us; the launch traced here: 59.7 us
  Pallas kernels  47.5 us (79%)
  local copies, waits for them, and re-layouts  8.7 us (14%)
  matrix products  1.79 us (3%)
  other arithmetic  1.1 us (2%)
  between operations  0.66 us (1%)
    pallas_call x1, Pallas kernels, per_device(): pl.pallas_call(functools.partial(kernel, ns, nb), out_shape=(jax.ShapeDty...  47.5 us
    unnamed x15, local copies, waits for them, and re-layouts  8.7 us
    dot_general x1, matrix products, per_device(): grad = lax.dot_general(xx, cc, TN, preferred_element_type=f32)  1.79 us

profile of v4, /device:TPU:0, one launch (start us, length us, event | category | flops | bytes accessed | tf_op | source)
XLA Modules:
  0.0 59.7 jit_solution(2343770666052758103)
XLA Ops:
  0.6 0.0 copy-start
  0.6 1.6 %copy-done = f32[1,1024,512]{2,1,0:T(8,128)S(1)} copy-done((f32[1,1024,512]{2,1,0:T(8,128)S(1)}, f32[1,1024,512]{2,1,0:T(8,128)}, u32[]{:S(2)}) %copy-start) | copy-done | bytes 2097176
  2.2 0.0 copy-start.1
  2.2 1.6 %copy-done.1 = bf16[2,1,1024,512]{3,2,1,0:T(8,128)(2,1)S(1)} copy-done((bf16[2,1,1024,512]{3,2,1,0:T(8,128)(2,1)S(1)}, bf16[2,1,1024,512]{3,2,1,0:T(8,128)(2,1)}, u32[]{:S(2)}) %copy-start.1) | copy-done | bytes 2097176
  3.8 0.0 copy-start.2
  3.8 1.2 %copy-done.2 = f32[1,512,512]{2,1,0:T(8,128)S(1)} copy-done((f32[1,512,512]{2,1,0:T(8,128)S(1)}, f32[1,512,512]{2,1,0:T(8,128)}, u32[]{:S(2)}) %copy-start.2) | copy-done | bytes 1048600
  5.0 0.0 copy-start.3
  5.0 1.2 %copy-done.3 = bf16[2,1,512,512]{3,2,1,0:T(8,128)(2,1)S(1)} copy-done((bf16[2,1,512,512]{3,2,1,0:T(8,128)(2,1)S(1)}, bf16[2,1,512,512]{3,2,1,0:T(8,128)(2,1)}, u32[]{:S(2)}) %copy-start.3) | copy-done | bytes 1048600
  6.3 0.0 copy-start.4
  6.3 0.9 %copy-done.4 = bf16[1,64,1024]{2,1,0:T(8,128)(2,1)S(1)} copy-done((bf16[1,64,1024]{2,1,0:T(8,128)(2,1)S(1)}, bf16[1,64,1024]{2,1,0:T(8,128)(2,1)}, u32[]{:S(2)}) %copy-start.4) | copy-done | bytes 131096
  7.2 0.0 copy-start.5
  7.2 0.8 %copy-done.5 = bf16[1,64,512]{2,1,0:T(8,128)(2,1)S(1)} copy-done((bf16[1,64,512]{2,1,0:T(8,128)(2,1)S(1)}, bf16[1,64,512]{2,1,0:T(8,128)(2,1)}, u32[]{:S(2)}) %copy-start.5) | copy-done | bytes 65560
  8.0 0.0 copy-start.6
  8.0 0.7 %copy-done.6 = s32[2,1,128]{2,1,0:T(1,128)S(1)} copy-done((s32[2,1,128]{2,1,0:T(1,128)S(1)}, s32[2,1,128]{2,1,0:T(1,128)}, u32[]{:S(2)}) %copy-start.6) | copy-done | bytes 1048
  8.7 47.5 %shard_map.94 = (bf16[1024,512]{1,0:T(8,128)(2,1)S(1)}, bf16[256,1024]{1,0:T(8,128)(2,1)S(1)}, bf16[256,512]{1,0:T(8,128)(2,1)S(1)}, bf16[512,512]{1,0:T(8,128)(2,1)S(1)}, bf16[128,512]{1,0:T(8,128)(2,1)S(1)}) custom-call(bf16[64,1024]{1,0:T(8,128)(2,1)S(1)} %bitcast.18, bf16[64,512]{1,0:T(8,128)(2,1)S(1)} %bitcast.20, s32[2,1,128]{2,1,0:T(1,128)S(1)} %copy-done.6, ...), custom_call_target="tpu_custom_call" | custom-call | tf_op jit(solution)/shard_map/pallas_call | solution.py:188
  56.2 1.8 %subtract_bitcast_fusion = f32[1,1024,512]{2,1,0:T(8,128)} fusion(bf16[1024,512]{1,0:T(8,128)(2,1)S(1)} %get-tuple-element.8, bf16[256,1024]{1,0:T(8,128)(2,1)S(1)} %get-tuple-element.9, bf16[256,512]{1,0:T(8,128)(2,1)S(1)} %get-tuple-element.10), kind=kOutput, calls=%fused_computation | convolution fusion | flops 270008320 | bytes 3932160 | tf_op jit(solution)/shard_map/dot_general | solution.py:224
  58.0 1.1 %bitcast_convert_fusion = f32[1,512,512]{2,1,0:T(8,128)} fusion(bf16[512,512]{1,0:T(8,128)(2,1)S(1)} %get-tuple-element.11), kind=kLoop, calls=%fused_computation.1 | loop fusion | flops 262144 | bytes 1572864 | tf_op jit(solution)/shard_map/broadcast_in_dim | solution.py:226
  59.1 0.7 %copy.11 = bf16[1,128,512]{2,1,0:T(8,128)(2,1)} copy(bf16[1,128,512]{2,1,0:T(8,128)(2,1)S(1)} %bitcast.19) | data formatting | bytes 262144
Async XLA Ops:
  0.6 1.6 %copy-start = (f32[1,1024,512]{2,1,0:T(8,128)S(1)}, f32[1,1024,512]{2,1,0:T(8,128)}, u32[]{:S(2)}) copy-start(f32[1,1024,512]{2,1,0:T(8,128)} %param.10) | copy-start | bytes 6291460
  2.2 1.6 %copy-start.1 = (bf16[2,1,1024,512]{3,2,1,0:T(8,128)(2,1)S(1)}, bf16[2,1,1024,512]{3,2,1,0:T(8,128)(2,1)}, u32[]{:S(2)}) copy-start(bf16[2,1,1024,512]{3,2,1,0:T(8,128)(2,1)} %param.12) | copy-start | bytes 6291460
  3.8 1.2 %copy-start.2 = (f32[1,512,512]{2,1,0:T(8,128)S(1)}, f32[1,512,512]{2,1,0:T(8,128)}, u32[]{:S(2)}) copy-start(f32[1,512,512]{2,1,0:T(8,128)} %param.11) | copy-start | bytes 3145732
  5.0 1.2 %copy-start.3 = (bf16[2,1,512,512]{3,2,1,0:T(8,128)(2,1)S(1)}, bf16[2,1,512,512]{3,2,1,0:T(8,128)(2,1)}, u32[]{:S(2)}) copy-start(bf16[2,1,512,512]{3,2,1,0:T(8,128)(2,1)} %param.13) | copy-start | bytes 3145732
  6.3 0.9 %copy-start.4 = (bf16[1,64,1024]{2,1,0:T(8,128)(2,1)S(1)}, bf16[1,64,1024]{2,1,0:T(8,128)(2,1)}, u32[]{:S(2)}) copy-start(bf16[1,64,1024]{2,1,0:T(8,128)(2,1)} %param.7) | copy-start | bytes 393220
  7.2 0.8 %copy-start.5 = (bf16[1,64,512]{2,1,0:T(8,128)(2,1)S(1)}, bf16[1,64,512]{2,1,0:T(8,128)(2,1)}, u32[]{:S(2)}) copy-start(bf16[1,64,512]{2,1,0:T(8,128)(2,1)} %param.8) | copy-start | bytes 196612
  8.0 0.7 %copy-start.6 = (s32[2,1,128]{2,1,0:T(1,128)S(1)}, s32[2,1,128]{2,1,0:T(1,128)}, u32[]{:S(2)}) copy-start(s32[2,1,128]{2,1,0:T(1,128)} %picks.1) | copy-start | bytes 3076

commit v5 on v3

--- a/solution.py
+++ b/solution.py
@@ -111,13 +111,6 @@
             )
             for k in range(1, nb)
         ]
-        if step == 0:
-            passed.wait_recv()
-            hops += [
-                remote(x_out.at[slot(0)], x_out.at[slot(k)], fs_sem.at[k], fr_sem.at[k], peers[k])
-                for k in range(1, nb)
-            ]
-
         @pl.loop(0, w2.shape[0], step=32)
         def _(r):
             part = pl.ds(r, 32)
@@ -167,6 +160,12 @@
         else:
             m2send[...] = final_two.astype(bf16)
             hops.append(remote(m2send, m2_out, hs_sem.at[6], hr_sem.at[6], nxt))
+    passed.wait_recv()
+    hops += [
+        remote(x_out.at[slot(0)], x_out.at[slot(k)], fs_sem.at[k], fr_sem.at[k], peers[k])
+        for k in range(1, nb)
+    ]
+
     for copy in hops:
         copy.wait_recv()
     for copy in sends:

time: 55.1 us -> 49 us (0.89)
  Pallas kernels: 49.2 us -> 43.1 us
    pallas_call x1, Pallas kernels: 49.2 us -> 43.1 us  [per_device(): pl.pallas_call(functools.partial(kernel, ns, nb), out_shape=(jax.ShapeDty...]
where the time goes in v5:
time: 49 us; the launch traced here: 48.9 us
  Pallas kernels  43.1 us (88%)
  matrix products  3.32 us (7%)
  other arithmetic  1.1 us (2%)
  local copies, waits for them, and re-layouts  0.66 us (1%)
  between operations  0.66 us (1%)
    pallas_call x1, Pallas kernels, per_device(): pl.pallas_call(functools.partial(kernel, ns, nb), out_shape=(jax.ShapeDty...  43.1 us
    dot_general x1, matrix products, per_device(): grad = lax.dot_general(xx, cc, TN, preferred_element_type=f32)  3.32 us
    broadcast_in_dim x1, other arithmetic, per_device(): return (moved_a[None], m2.astype(f32)[None], errs[None])  1.1 us

profile of v5, /device:TPU:0, one launch (start us, length us, event | category | flops | bytes accessed | tf_op | source)
XLA Modules:
  0.0 48.9 jit_solution(4206836274603792463)
XLA Ops:
  0.6 43.1 %shard_map.94 = (bf16[1024,512]{1,0:T(8,128)(2,1)}, bf16[256,1024]{1,0:T(8,128)(2,1)}, bf16[256,512]{1,0:T(8,128)(2,1)}, bf16[512,512]{1,0:T(8,128)(2,1)}, bf16[128,512]{1,0:T(8,128)(2,1)}) custom-call(bf16[64,1024]{1,0:T(8,128)(2,1)} %bitcast.18, bf16[64,512]{1,0:T(8,128)(2,1)} %bitcast.20, s32[2,1,128]{2,1,0:T(1,128)} %picks.1, f32[1024,512]{1,0:T(8,128)} %bitcast.14, ...), custom_call_target="tpu_custom_call" | custom-call | tf_op jit(solution)/shard_map/pallas_call | solution.py:187
  43.8 0.0 copy-start
  43.8 0.0 copy-start.1
  43.8 3.3 %subtract_bitcast_fusion = f32[1,1024,512]{2,1,0:T(8,128)} fusion(bf16[1024,512]{1,0:T(8,128)(2,1)} %get-tuple-element.8, bf16[256,1024]{1,0:T(8,128)(2,1)} %get-tuple-element.9, bf16[256,512]{1,0:T(8,128)(2,1)} %get-tuple-element.10), kind=kOutput, calls=%fused_computation | convolution fusion | flops 270008320 | bytes 3932160 | tf_op jit(solution)/shard_map/dot_general | solution.py:223
  47.1 0.0 copy-done
  47.1 1.1 %bitcast_convert_fusion = f32[1,512,512]{2,1,0:T(8,128)} fusion(bf16[512,512]{1,0:T(8,128)(2,1)S(1)} %copy-done), kind=kLoop, calls=%fused_computation.1 | loop fusion | flops 262144 | bytes 1572864 | tf_op jit(solution)/shard_map/broadcast_in_dim | solution.py:225
  48.2 0.0 copy-done.1
  48.2 0.7 %copy.11 = bf16[1,128,512]{2,1,0:T(8,128)(2,1)} copy(bf16[1,128,512]{2,1,0:T(8,128)(2,1)S(1)} %bitcast.19) | data formatting | bytes 262144
Async XLA Ops:
  43.8 3.3 %copy-start = (bf16[512,512]{1,0:T(8,128)(2,1)S(1)}, bf16[512,512]{1,0:T(8,128)(2,1)}, u32[]{:S(2)}) copy-start(bf16[512,512]{1,0:T(8,128)(2,1)} %get-tuple-element.11) | copy-start | bytes 1572868
  43.8 4.4 %copy-start.1 = (bf16[128,512]{1,0:T(8,128)(2,1)S(1)}, bf16[128,512]{1,0:T(8,128)(2,1)}, u32[]{:S(2)}) copy-start(bf16[128,512]{1,0:T(8,128)(2,1)} %get-tuple-element.12) | copy-start | bytes 393220

commit v6 on v5

--- a/solution.py
+++ b/solution.py
@@ -42,6 +42,8 @@
         pairs += [(l1.at[piece], w1.at[piece])]
         pairs += [(n1h.at[i, piece], n1.at[i, piece]) for i in range(STEPS)]
     pairs += [(l2, w2)] + [(n2h.at[i], n2.at[i]) for i in range(STEPS)]
+    order = [0, 3, 6, 9, 12, 1, 2, 4, 5, 7, 8, 10, 11, 13, 14]
+    pairs = [pairs[i] for i in order]
     loads = [
         pltpu.make_async_copy(src, dst, load_sem.at[i]) for i, (src, dst) in enumerate(pairs)
     ]
@@ -78,21 +80,13 @@
 
     hops = []
     for q in range(4):
-        for load in loads[3 * q : 3 * q + 3]:
-            load.wait()
+        loads[q].wait()
 
         @pl.loop(0, quarter, step=32)
         def _(r, q=q):
             part = pl.ds(q * quarter + r, 32)
-            w = w1[part, :]
-            w1b[part, :] = w.astype(bf16)
-            w = keep * w + root_step * n1[0, part, :].astype(f32)
-            w1[part, :] = w
-            dsend[part, :] = (keep * w + root_step * n1[1, part, :].astype(f32)).astype(bf16)
-        piece = pl.ds(q * quarter, quarter)
-        hops.append(remote(dsend.at[piece], d_out.at[piece], hs_sem.at[q], hr_sem.at[q], nxt))
-    for load in loads[12:]:
-        load.wait()
+            w1b[part, :] = w1[part, :].astype(bf16)
+    loads[4].wait()
     for copy in gathers:
         copy.wait_recv()
 
@@ -111,6 +105,23 @@
             )
             for k in range(1, nb)
         ]
+        if step == 0:
+            for q in range(4):
+                for load in loads[5 + 2 * q : 7 + 2 * q]:
+                    load.wait()
+
+                @pl.loop(0, quarter, step=32)
+                def _(r, q=q):
+                    part = pl.ds(q * quarter + r, 32)
+                    w = w1[part, :]
+                    w = keep * w + root_step * n1[0, part, :].astype(f32)
+                    w1[part, :] = w
+                    dsend[part, :] = (keep * w + root_step * n1[1, part, :].astype(f32)).astype(bf16)
+                piece = pl.ds(q * quarter, quarter)
+                hops.append(remote(dsend.at[piece], d_out.at[piece], hs_sem.at[q], hr_sem.at[q], nxt))
+            for load in loads[13:]:
+                load.wait()
+
         @pl.loop(0, w2.shape[0], step=32)
         def _(r):
             part = pl.ds(r, 32)

time: 49 us -> 49.5 us (1.010)
  Pallas kernels: 43.1 us -> 43.6 us
where the time goes in v6:
time: 49.5 us; the launch traced here: 49.3 us
  Pallas kernels  43.6 us (88%)
  matrix products  3.32 us (7%)
  other arithmetic  1.1 us (2%)
  local copies, waits for them, and re-layouts  0.66 us (1%)
  between operations  0.66 us (1%)
    pallas_call x1, Pallas kernels, per_device(): pl.pallas_call(functools.partial(kernel, ns, nb), out_shape=(jax.ShapeDty...  43.6 us
    dot_general x1, matrix products, per_device(): grad = lax.dot_general(xx, cc, TN, preferred_element_type=f32)  3.32 us
    broadcast_in_dim x1, other arithmetic, per_device(): return (moved_a[None], m2.astype(f32)[None], errs[None])  1.1 us

profile of v6, /device:TPU:0, one launch (start us, length us, event | category | flops | bytes accessed | tf_op | source)
XLA Modules:
  0.0 49.3 jit_solution(16266725882436343887)
XLA Ops:
  0.6 43.6 %shard_map.94 = (bf16[1024,512]{1,0:T(8,128)(2,1)}, bf16[256,1024]{1,0:T(8,128)(2,1)}, bf16[256,512]{1,0:T(8,128)(2,1)}, bf16[512,512]{1,0:T(8,128)(2,1)}, bf16[128,512]{1,0:T(8,128)(2,1)}) custom-call(bf16[64,1024]{1,0:T(8,128)(2,1)} %bitcast.18, bf16[64,512]{1,0:T(8,128)(2,1)} %bitcast.20, s32[2,1,128]{2,1,0:T(1,128)} %picks.1, f32[1024,512]{1,0:T(8,128)} %bitcast.14, ...), custom_call_target="tpu_custom_call" | custom-call | tf_op jit(solution)/shard_map/pallas_call | solution.py:198
  44.2 0.0 copy-start
  44.3 0.0 copy-start.1
  44.3 3.3 %subtract_bitcast_fusion = f32[1,1024,512]{2,1,0:T(8,128)} fusion(bf16[1024,512]{1,0:T(8,128)(2,1)} %get-tuple-element.8, bf16[256,1024]{1,0:T(8,128)(2,1)} %get-tuple-element.9, bf16[256,512]{1,0:T(8,128)(2,1)} %get-tuple-element.10), kind=kOutput, calls=%fused_computation | convolution fusion | flops 270008320 | bytes 3932160 | tf_op jit(solution)/shard_map/dot_general | solution.py:234
  47.6 0.0 copy-done
  47.6 1.1 %bitcast_convert_fusion = f32[1,512,512]{2,1,0:T(8,128)} fusion(bf16[512,512]{1,0:T(8,128)(2,1)S(1)} %copy-done), kind=kLoop, calls=%fused_computation.1 | loop fusion | flops 262144 | bytes 1572864 | tf_op jit(solution)/shard_map/broadcast_in_dim | solution.py:236
  48.7 0.0 copy-done.1
  48.7 0.7 %copy.11 = bf16[1,128,512]{2,1,0:T(8,128)(2,1)} copy(bf16[1,128,512]{2,1,0:T(8,128)(2,1)S(1)} %bitcast.19) | data formatting | bytes 262144
Async XLA Ops:
  44.2 3.3 %copy-start = (bf16[512,512]{1,0:T(8,128)(2,1)S(1)}, bf16[512,512]{1,0:T(8,128)(2,1)}, u32[]{:S(2)}) copy-start(bf16[512,512]{1,0:T(8,128)(2,1)} %get-tuple-element.11) | copy-start | bytes 1572868
  44.3 4.4 %copy-start.1 = (bf16[128,512]{1,0:T(8,128)(2,1)S(1)}, bf16[128,512]{1,0:T(8,128)(2,1)}, u32[]{:S(2)}) copy-start(bf16[128,512]{1,0:T(8,128)(2,1)} %get-tuple-element.12) | copy-start | bytes 393220
